TPU v7x, 512 devices: a whole 4x8x8 slice. The times are simulated.
512 devices in a mesh: dp: 8 (over y), feat: 64 (over x, z, core).
Axes of the slice: x: 4, y: 8, z: 8, core: 2. Of those that a mesh axis runs over, the one named last changes fastest.
Arguments:
- features: bfloat16 [8, 16384, 128], P('dp', None, 'feat'), may hold values from -6 to 6
- tile_weights: bfloat16 [8, 1536, 128, 128], P('dp', 'feat'), may hold values from -0.15625 to 0.15625
- tile_rows: int32 [8, 1536], P('dp', 'feat'), may hold values from 0 to 1
- tile_owners: int32 [8, 1536, 1], P('dp', 'feat'), may hold values from 0 to 63; in each aligned block of 24 rows (0 to 23, 24 to 47, ..., all dimensions but the last counted through in order) at most 2 rows name the same one
- tile_blocks: int32 [8, 1536], P('dp', 'feat'), may hold values from 0 to 1
- tile_counts: int32 [8, 64], P('dp', 'feat'), may hold values from 6 to 24, as said below
- cotangent: bfloat16 [8, 16384, 1024], P('dp', 'feat'), may hold values from -0.046875 to 0.046875
- w_self: bfloat16 [128, 1024], replicated, may hold values from -0.5 to 0.5
- w_neigh: bfloat16 [128, 1024], replicated, may hold values from -0.5 to 0.5
- bias: float32 [1024], replicated, may hold values from -4 to 4
Outputs:
- grad_self: float32 [128, 1024], P(None, 'feat')
- grad_neigh: float32 [128, 1024], P(None, 'feat')
- grad_bias: float32 [1024], P('feat')
Inputs may be any that keep to these rules, and one draw needn't show every extreme that they name: `tile_owners`: among the 24 tile slots of one device at most 2 name one owner, a bound that some block of them reaches. `tile_counts`: in every batch some device has all 24 slots live.
All inputs are finite; a program needn't handle non-finite values.
Results may differ from a plain program's by a relative error of at most 0.008.
Values may be sent and summed in bfloat16 or wider, within the bound.
No kernel may reach another device: no remote copies, remote signals or barrier semaphores. Data moves between devices by JAX's collectives and lax.ppermute only.
A program may use at most 64 MiB of HBM per device.

v0:
```python
import jax
import jax.numpy as jnp
from jax import lax
from jax.sharding import PartitionSpec as P


def silu_slope(pre_act):
    sigmoid_z = jax.nn.sigmoid(pre_act)
    return sigmoid_z * (1.0 + pre_act * (1.0 - sigmoid_z))


def local(
    features,
    tile_weights,
    tile_rows,
    tile_owners,
    tile_blocks,
    tile_counts,
    cotangent,
    w_self,
    w_neigh,
    bias,
):
    owned = lax.all_to_all(features, "feat", split_axis=1, concat_axis=2, tiled=True)[0]
    node_rows, feat_width = owned.shape
    slot_count = tile_weights.shape[1]
    tile_side = tile_weights.shape[2]
    row_blocks = node_rows // tile_side
    peer_count = lax.axis_size("feat")
    row_index = tile_rows[0]
    owner_index = tile_owners[0, :, 0]
    block_index = tile_blocks[0]
    live = jnp.arange(slot_count, dtype=jnp.int32) < tile_counts[0, 0]
    whole = lax.all_gather(owned, "feat", axis=0, tiled=True)
    picked = whole.reshape(-1, tile_side, feat_width)[owner_index * row_blocks + block_index]
    products = jnp.einsum(
        "kij,kjf->kif", tile_weights[0], picked, preferred_element_type=jnp.float32
    )
    select = (
        (row_index[None, :] == jnp.arange(row_blocks, dtype=jnp.int32)[:, None]) & live[None, :]
    ).astype(jnp.float32)
    summed = jnp.einsum("rk,kif->rif", select, products, precision=lax.Precision.HIGHEST)
    neighbour = summed.reshape(node_rows, feat_width).astype(jnp.bfloat16)
    pre_act = (
        jnp.dot(owned, w_self, preferred_element_type=jnp.float32)
        + jnp.dot(neighbour, w_neigh, preferred_element_type=jnp.float32)
        + bias
    )
    slope = (cotangent[0].astype(jnp.float32) * silu_slope(pre_act)).astype(jnp.bfloat16)
    grad_s = jnp.einsum("nf,nh->fh", owned, slope, preferred_element_type=jnp.float32)
    grad_n = jnp.einsum("nf,nh->fh", neighbour, slope, preferred_element_type=jnp.float32)
    grad_b = jnp.sum(slope.astype(jnp.float32), axis=0)
    total_s, total_n, total_b = lax.psum((grad_s, grad_n, grad_b), ("dp", "feat"))
    column_count = w_self.shape[1] // peer_count
    start = lax.axis_index("feat") * column_count
    out_s = lax.dynamic_slice_in_dim(total_s, start, column_count, 1)
    out_n = lax.dynamic_slice_in_dim(total_n, start, column_count, 1)
    out_b = lax.dynamic_slice_in_dim(total_b, start, column_count, 0)
    return (out_s, out_n, out_b)


def solution(mesh):
    return jax.shard_map(
        local,
        mesh=mesh,
        in_specs=(
            P("dp", None, "feat"),
            P("dp", "feat", None, None),
            P("dp", "feat"),
            P("dp", "feat", None),
            P("dp", "feat"),
            P("dp", "feat"),
            P("dp", "feat", None),
            P(),
            P(),
            P(),
        ),
        out_specs=(P(None, "feat"), P(None, "feat"), P("feat")),
        check_vma=False,
    )
```

profile of v0, /device:TPU:23, one launch (start us, length us, event | category | flops | bytes accessed | tf_op | source)
XLA Modules:
  0.0 554.2 jit_solution(6314317441695136422)
XLA Ops:
  7.2 15.4 %copy.26 = bf16[1,16384,2]{2,0,1:T(2,128)(2,1)} copy(bf16[1,16384,2]{1,2,0:T(2,128)(2,1)} %param.10) | data formatting | bytes 131072 | tf_op args[0]
  22.6 0.5 broadcast.52
  23.1 90.8 %reduce = bf16[16384,2]{1,0:T(8,128)(2,1)} reduce(bf16[16384,1,2]{2,1,0:T(2,128)(2,1)} %bitcast.51, bf16[]{:T(256)} %broadcast.52), dimensions={1}, to_apply=%bitcast.36.reduce_sub_computation | reduce | bytes 131074
  113.9 7.1 %reshape.61 = bf16[64,2,256]{2,1,0:T(2,128)(2,1)S(1)} reshape(bf16[16384,2]{1,0:T(8,128)(2,1)} %reduce) | data formatting | bytes 131072
  121.0 21.9 %all_to_all.15 = bf16[64,2,256]{2,1,0:T(2,128)(2,1)S(1)} all-to-all(bf16[64,2,256]{2,1,0:T(2,128)(2,1)S(1)} %reshape.61), channel_id=1, replica_groups=mesh['dp'=8,'feat'=64] {'feat'}, dimensions={0} | all-to-all | bytes 131072 | tf_op jit(solution)/shard_map/all_to_all | solution.py:24
  142.9 16.4 %reshape.62 = bf16[16384,1,2]{2,1,0:T(2,128)(2,1)} reshape(bf16[64,2,256]{2,1,0:T(2,128)(2,1)S(1)} %all_to_all.15) | data formatting | bytes 131072
  159.3 15.4 %copy.27 = bf16[1,16384,2]{1,2,0:T(2,128)(2,1)S(1)} copy(bf16[1,16384,2]{2,0,1:T(2,128)(2,1)} %bitcast.52) | data formatting | bytes 131072 | tf_op jit(solution)/shard_map/all_to_all | solution.py:24
  174.7 0.1 copy.28
  174.8 0.7 squeeze.14
  175.5 0.2 all-reduce.3.cloned.1.call-start
  176.4 1.2 fusion.10
  177.6 77.5 %all-gather.2.cloned.1.call-done = bf16[16384,128]{0,1:T(8,128)(2,1)} async-done(((bf16[256,128]{0,1:T(8,128)(2,1)}), bf16[16384,128]{0,1:T(8,128)(2,1)}) %all-gather.2.cloned.1.call-update) | async-done | bytes 4194320 | tf_op jit(solution)/shard_map/all_gather | solution.py:34
  255.0 6.4 %copy.29 = bf16[16384,128]{1,0:T(8,128)(2,1)} copy(bf16[16384,128]{0,1:T(8,128)(2,1)} %all-gather.2.cloned.1.call-done) | data formatting | bytes 8388608 | tf_op jit(solution)/shard_map/all_gather | solution.py:34
  261.4 2.9 gather_fusion
  264.4 1.9 convolution_bitcast_fusion
  266.2 2.0 copy.31
  268.2 0.6 convolution_convert_fusion
  268.9 1.8 convert_reduce_fusion
  270.6 1.1 fusion.11
  271.8 1.1 convolution_bitcast_fusion.1
  272.9 96.3 %psum.23 = f32[1024]{0:T(1024)S(1)} all-reduce(f32[1024]{0:T(1024)S(1)} %get-tuple-element.5), channel_id=1, replica_groups=mesh['dp'=8,'feat'=64] {'dp','feat'}, use_global_device_ids=true, to_apply=%region_3.0 | all-reduce | flops 1024 | bytes 8192 | tf_op jit(solution)/shard_map/psum | solution.py:53
  369.3 0.6 dynamic_slice.11
  369.9 176.2 %all-reduce.3.cloned.1.call-done = (f32[128,1024]{0,1:T(8,128)}, f32[128,1024]{0,1:T(8,128)}) async-done(((f32[128,1024]{0,1:T(8,128)}, f32[128,1024]{0,1:T(8,128)}), (f32[128,1024]{0,1:T(8,128)}, f32[128,1024]{0,1:T(8,128)})) %all-reduce.3.cloned.1.call-update) | async-done | bytes 1048592 | tf_op jit(solution)/shard_map/psum | solution.py:53
  546.0 1.3 constant_dynamic-slice_fusion
  (22 shorter events, 0.1 us)
Async XLA Ops:
  7.2 257.2 %copy-start = (bf16[1,24,128,128]{3,2,1,0:T(8,128)(2,1)S(1)}, bf16[1,24,128,128]{3,2,1,0:T(8,128)(2,1)}, u32[]{:S(2)}) copy-start(bf16[1,24,128,128]{3,2,1,0:T(8,128)(2,1)} %param.11) | copy-start | bytes 2359300
  7.2 247.8 %all-gather.2.cloned.1.call-start = ((), (), s32[]{:S(2)}) async-start(), calls=%async_computation.1 | async-start | bytes 4259840 | tf_op jit(solution)/shard_map/all_gather | solution.py:34
  159.3 17.1 %copy-start.5 = (s32[1,24]{1,0:T(1,128)S(1)}, s32[1,24]{1,0:T(1,128)}, u32[]{:S(2)}) copy-start(s32[1,24]{1,0:T(1,128)} %param.14) | copy-start | bytes 292
  159.3 17.1 %copy-start.6 = (s32[1,24,1]{1,2,0:T(1,128)S(1)}, s32[1,24,1]{1,2,0:T(1,128)}, u32[]{:S(2)}) copy-start(s32[1,24,1]{1,2,0:T(1,128)} %param.13) | copy-start | bytes 292
  159.3 17.1 %copy-start.2 = (bf16[128,1024]{1,0:T(8,128)(2,1)S(1)}, bf16[128,1024]{1,0:T(8,128)(2,1)}, u32[]{:S(2)}) copy-start(bf16[128,1024]{1,0:T(8,128)(2,1)} %param.17) | copy-start | bytes 786436
  175.5 370.6 %all-reduce.3.cloned.1.call-start = ((), (), s32[]{:S(2)}) async-start(), calls=%async_computation.2 | async-start | bytes 2097152 | tf_op jit(solution)/shard_map/psum | solution.py:53
  261.4 6.8 %copy-start.3 = (s32[1,24]{1,0:T(1,128)S(1)}, s32[1,24]{1,0:T(1,128)}, u32[]{:S(2)}) copy-start(s32[1,24]{1,0:T(1,128)} %param.12) | copy-start | bytes 292
  264.4 4.5 copy-start.4
  268.8 3.0 copy-start.1
Sparse Core Ops, SparseCore 0:
  175.6 79.3 all-gather.1
  273.1 272.9 all-reduce.2
where the time goes:
time: 556 us; the launch traced here: 554 us
  waiting for transfers between devices  254 us (46%)
  blocking collectives  118 us (21%)
  other arithmetic  90.8 us (16%)
  local copies, waits for them, and re-layouts  68.7 us (12%)
  between operations  14.9 us (3%)
  matrix products  7.67 us (1%)
    psum x1, waiting for transfers between devices, local(): lax.psum((grad_s, grad_n, grad_b), ('dp', 'feat'))  176 us
    psum x1, blocking collectives, local(): lax.psum((grad_s, grad_n, grad_b), ('dp', 'feat'))  96.3 us
    unnamed x1, other arithmetic  90.8 us
    all_gather x1, waiting for transfers between devices, local(): whole = lax.all_gather(owned, 'feat', axis=0, tiled=True)  77.5 us
    unnamed x19, local copies, waits for them, and re-layouts  39.5 us
    all_to_all x1, blocking collectives, local(): lax.all_to_all(features, 'feat', split_axis=1, concat_axis=2, tiled=True)[0]  21.9 us
    all_to_all x2, local copies, waits for them, and re-layouts, local(): lax.all_to_all(features, 'feat', split_axis=1, concat_axis=2, tiled=True)[0]  15.5 us
  transfers between devices with their start and end apart: 2, of which 2 were waited for; matrix products, arithmetic and copies ran while one was open for 0% of the time, Pallas kernels for 0%

commit v1 on v0

--- a/solution.py
+++ b/solution.py
@@ -31,7 +31,20 @@
     owner_index = tile_owners[0, :, 0]
     block_index = tile_blocks[0]
     live = jnp.arange(slot_count, dtype=jnp.int32) < tile_counts[0, 0]
-    whole = lax.all_gather(owned, "feat", axis=0, tiled=True)
+    n_now = lax.axis_size("feat")
+    view_out, s_next = (n_now, lax.axis_index("feat"))
+    whole, prior = (owned, 1)
+    while prior < view_out:
+        fields = []
+        tick = 0
+        while tick < view_out:
+            fields.append((tick, tick ^ prior))
+            tick += 1
+        arr_out = lax.ppermute(whole, "feat", fields)
+        block_out = jnp.concatenate([whole, arr_out], axis=0)
+        block_next = jnp.concatenate([arr_out, whole], axis=0)
+        whole = jnp.where(s_next & prior == 0, block_out, block_next)
+        prior = 2 * prior
     picked = whole.reshape(-1, tile_side, feat_width)[owner_index * row_blocks + block_index]
     products = jnp.einsum(
         "kij,kjf->kif", tile_weights[0], picked, preferred_element_type=jnp.float32

time: 556 us -> 615 us (1.11)
  waiting for transfers between devices: 254 us -> 283 us
  starting transfers between devices: 0.26 us -> 15.9 us
  other arithmetic: 90.8 us -> 98.5 us
  blocking collectives: 118 us -> 125 us
    ppermute x0 -> x6, waiting for transfers between devices: none -> 109 us  [local(): arr_out = lax.ppermute(whole, 'feat', fields)]
    all_gather x1 -> x0, waiting for transfers between devices: 77.5 us -> none  [local(): whole = lax.all_gather(owned, 'feat', axis=0, tiled=True)]
    ppermute x0 -> x6, starting transfers between devices: none -> 15.9 us  [local(): arr_out = lax.ppermute(whole, 'feat', fields)]
    select_n x0 -> x6, other arithmetic: none -> 7.73 us  [local(): whole = jnp.where(s_next & prior == 0, block_out, block_next)]
    psum x1, blocking collectives: 96.3 us -> 103 us  [local(): lax.psum((grad_s, grad_n, grad_b), ('dp', 'feat'))]
    all_gather x1 -> x0, local copies, waits for them, and re-layouts: 6.42 us -> none  [local(): whole = lax.all_gather(owned, 'feat', axis=0, tiled=True)]
    select_n x0 -> x1, local copies, waits for them, and re-layouts: none -> 6.41 us  [local(): whole = jnp.where(s_next & prior == 0, block_out, block_next)]
    unnamed x19 -> x21, local copies, waits for them, and re-layouts: 39.5 us -> 39.5 us
  transfers between devices with their start and end apart: 2 -> 7, of which waited for: 2 -> 7; matrix products, arithmetic and copies ran while one was open for 0% -> 0% of each run, Pallas kernels for 0% -> 0%
where the time goes in v1:
time: 615 us; the launch traced here: 613 us
  waiting for transfers between devices  283 us (46%)
  blocking collectives  125 us (20%)
  other arithmetic  98.5 us (16%)
  local copies, waits for them, and re-layouts  68.1 us (11%)
  starting transfers between devices  15.9 us (3%)
  between operations  15 us (2%)
  matrix products  7.91 us (1%)
    psum x1, waiting for transfers between devices, local(): lax.psum((grad_s, grad_n, grad_b), ('dp', 'feat'))  175 us
    ppermute x6, waiting for transfers between devices, local(): arr_out = lax.ppermute(whole, 'feat', fields)  109 us
    psum x1, blocking collectives, local(): lax.psum((grad_s, grad_n, grad_b), ('dp', 'feat'))  103 us
    unnamed x1, other arithmetic  90.8 us
    unnamed x21, local copies, waits for them, and re-layouts  39.5 us
    all_to_all x1, blocking collectives, local(): lax.all_to_all(features, 'feat', split_axis=1, concat_axis=2, tiled=True)[0]  21.9 us
    ppermute x6, starting transfers between devices, local(): arr_out = lax.ppermute(whole, 'feat', fields)  15.9 us
    all_to_all x2, local copies, waits for them, and re-layouts, local(): lax.all_to_all(features, 'feat', split_axis=1, concat_axis=2, tiled=True)[0]  15.4 us
  transfers between devices with their start and end apart: 7, of which 7 were waited for; matrix products, arithmetic and copies ran while one was open for 0% of the time, Pallas kernels for 0%

profile of v1, /device:TPU:23, one launch (start us, length us, event | category | flops | bytes accessed | tf_op | source)
XLA Modules:
  0.0 613.3 jit_solution(4694558539701994349)
XLA Ops:
  7.2 15.3 %copy.26 = bf16[1,16384,2]{2,0,1:T(2,128)(2,1)} copy(bf16[1,16384,2]{1,2,0:T(2,128)(2,1)} %param.10) | data formatting | bytes 131072 | tf_op args[0]
  23.1 90.8 %reduce = bf16[16384,2]{1,0:T(8,128)(2,1)} reduce(bf16[16384,1,2]{2,1,0:T(2,128)(2,1)} %bitcast.51, bf16[]{:T(256)} %broadcast.55), dimensions={1}, to_apply=%bitcast.36.reduce_sub_computation | reduce | bytes 131074
  113.8 7.1 %reshape.62 = bf16[64,2,256]{2,1,0:T(2,128)(2,1)S(1)} reshape(bf16[16384,2]{1,0:T(8,128)(2,1)} %reduce) | data formatting | bytes 131072
  121.0 21.9 %all_to_all.15 = bf16[64,2,256]{2,1,0:T(2,128)(2,1)S(1)} all-to-all(bf16[64,2,256]{2,1,0:T(2,128)(2,1)S(1)} %reshape.62), channel_id=1, replica_groups=mesh['dp'=8,'feat'=64] {'feat'}, dimensions={0} | all-to-all | bytes 131072 | tf_op jit(solution)/shard_map/all_to_all | solution.py:24
  142.9 16.4 %reshape.63 = bf16[16384,1,2]{2,1,0:T(2,128)(2,1)} reshape(bf16[64,2,256]{2,1,0:T(2,128)(2,1)S(1)} %all_to_all.15) | data formatting | bytes 131072
  159.3 15.3 %copy.27 = bf16[1,16384,2]{1,2,0:T(2,128)(2,1)S(1)} copy(bf16[1,16384,2]{2,0,1:T(2,128)(2,1)} %bitcast.52) | data formatting | bytes 131072 | tf_op jit(solution)/shard_map/all_to_all | solution.py:24
  174.8 2.3 collective-permute-start
  178.0 2.4 collective-permute-start.1
  180.5 4.2 collective-permute-done.1
  184.7 2.6 collective-permute-start.2
  187.3 13.8 %collective-permute-done.2 = bf16[1024,128]{0,1:T(8,128)(2,1)S(1)} collective-permute-done((bf16[1024,128]{0,1:T(8,128)(2,1)S(1)}, bf16[1024,128]{0,1:T(8,128)(2,1)S(1)}, u32[]{:S(2)}, u32[]{:S(2)}) %collective-permute-start.2) | collective-permute-done | bytes 262176 | tf_op jit(solution)/shard_map/ppermute | solution.py:43
  201.3 2.2 collective-permute-start.3
  203.5 25.0 %collective-permute-done.3 = bf16[2048,128]{0,1:T(8,128)(2,1)S(1)} collective-permute-done((bf16[2048,128]{0,1:T(8,128)(2,1)S(1)}, bf16[2048,128]{0,1:T(8,128)(2,1)S(1)}, u32[]{:S(2)}, u32[]{:S(2)}) %collective-permute-start.3) | collective-permute-done | bytes 524320 | tf_op jit(solution)/shard_map/ppermute | solution.py:43
  228.7 2.2 collective-permute-start.4
  231.0 22.8 %collective-permute-done.4 = bf16[4096,128]{0,1:T(8,128)(2,1)} collective-permute-done((bf16[4096,128]{0,1:T(8,128)(2,1)S(1)}, bf16[4096,128]{0,1:T(8,128)(2,1)}, u32[]{:S(2)}, u32[]{:S(2)}) %collective-permute-start.4) | collective-permute-done | bytes 1048608 | tf_op jit(solution)/shard_map/ppermute | solution.py:43
  253.8 2.7 maximum_select_fusion.1
  256.5 4.1 collective-permute-start.5
  262.7 41.9 %collective-permute-done.5 = bf16[8192,128]{0,1:T(8,128)(2,1)} collective-permute-done((bf16[8192,128]{0,1:T(8,128)(2,1)S(1)}, bf16[8192,128]{0,1:T(8,128)(2,1)}, u32[]{:S(2)}, u32[]{:S(2)}) %collective-permute-start.5) | collective-permute-done | bytes 2097184 | tf_op jit(solution)/shard_map/ppermute | solution.py:43
  304.6 4.5 maximum_select_fusion
  309.1 6.4 %copy.29 = bf16[16384,128]{1,0:T(8,128)(2,1)} copy(bf16[16384,128]{0,1:T(8,128)(2,1)} %maximum_select_fusion) | data formatting | bytes 8388608 | tf_op jit(solution)/shard_map/jit(_where)/select_n | solution.py:46
  315.5 2.9 gather_fusion
  320.3 2.0 copy.31
  327.1 103.0 %psum.23 = f32[1024]{0:T(1024)S(1)} all-reduce(f32[1024]{0:T(1024)S(1)} %get-tuple-element.5), channel_id=1, replica_groups=mesh['dp'=8,'feat'=64] {'dp','feat'}, use_global_device_ids=true, to_apply=%region_3.4 | all-reduce | flops 1024 | bytes 8192 | tf_op jit(solution)/shard_map/psum | solution.py:66
  430.6 174.5 %all-reduce.3.cloned.1.call-done = (f32[128,1024]{0,1:T(8,128)}, f32[128,1024]{0,1:T(8,128)}) async-done(((f32[128,1024]{0,1:T(8,128)}, f32[128,1024]{0,1:T(8,128)}), (f32[128,1024]{0,1:T(8,128)}, f32[128,1024]{0,1:T(8,128)})) %all-reduce.3.cloned.1.call-update) | async-done | bytes 1048592 | tf_op jit(solution)/shard_map/psum | solution.py:66
  (39 shorter events, 11.9 us)
Async XLA Ops:
  7.2 311.3 %copy-start = (bf16[1,24,128,128]{3,2,1,0:T(8,128)(2,1)S(1)}, bf16[1,24,128,128]{3,2,1,0:T(8,128)(2,1)}, u32[]{:S(2)}) copy-start(bf16[1,24,128,128]{3,2,1,0:T(8,128)(2,1)} %param.11) | copy-start | bytes 2359300
  7.2 598.0 %all-reduce.3.cloned.1.call-start = ((), (), s32[]{:S(2)}) async-start(), calls=%async_computation.1 | async-start | bytes 2097152 | tf_op jit(solution)/shard_map/psum | solution.py:66
  174.6 86.6 %copy-start.6 = (s32[1,24]{1,0:T(1,128)S(1)}, s32[1,24]{1,0:T(1,128)}, u32[]{:S(2)}) copy-start(s32[1,24]{1,0:T(1,128)} %param.14) | copy-start | bytes 292
  174.7 86.6 %copy-start.7 = (s32[1,24,1]{1,2,0:T(1,128)S(1)}, s32[1,24,1]{1,2,0:T(1,128)}, u32[]{:S(2)}) copy-start(s32[1,24,1]{1,2,0:T(1,128)} %param.13) | copy-start | bytes 292
  174.7 86.7 %copy-start.3 = (bf16[128,1024]{1,0:T(8,128)(2,1)S(1)}, bf16[128,1024]{1,0:T(8,128)(2,1)}, u32[]{:S(2)}) copy-start(bf16[128,1024]{1,0:T(8,128)(2,1)} %param.17) | copy-start | bytes 786436
  174.8 3.2 collective-permute-start
  178.0 6.6 %collective-permute-start.1 = (bf16[512,128]{0,1:T(8,128)(2,1)S(1)}, bf16[512,128]{0,1:T(8,128)(2,1)S(1)}, u32[]{:S(2)}, u32[]{:S(2)}) collective-permute-start(bf16[512,128]{0,1:T(8,128)(2,1)S(1)} %maximum_select_fusion.5), channel_id=1, source_target_pairs={{0,2},{1,3},{2,0},{3,1},{4,6},{5,7},{6,4},{7,5},{8,10},{9,11},{10,... | collective-permute-start | bytes 393224 | tf_op jit(solution)/shard_map/ppermute | solution.py:43
  184.7 16.4 %collective-permute-start.2 = (bf16[1024,128]{0,1:T(8,128)(2,1)S(1)}, bf16[1024,128]{0,1:T(8,128)(2,1)S(1)}, u32[]{:S(2)}, u32[]{:S(2)}) collective-permute-start(bf16[1024,128]{0,1:T(8,128)(2,1)S(1)} %maximum_select_fusion.4), channel_id=1, source_target_pairs={{0,4},{1,5},{2,6},{3,7},{4,0},{5,1},{6,2},{7,3},{8,12},{9,13},{10,... | collective-permute-start | bytes 786440 | tf_op jit(solution)/shard_map/ppermute | solution.py:43
  201.3 27.1 %collective-permute-start.3 = (bf16[2048,128]{0,1:T(8,128)(2,1)S(1)}, bf16[2048,128]{0,1:T(8,128)(2,1)S(1)}, u32[]{:S(2)}, u32[]{:S(2)}) collective-permute-start(bf16[2048,128]{0,1:T(8,128)(2,1)S(1)} %maximum_select_fusion.3), channel_id=1, source_target_pairs={{0,8},{1,9},{2,10},{3,11},{4,12},{5,13},{6,14},{7,15},{8,0},{9,1},... | collective-permute-start | bytes 1572872 | tf_op jit(solution)/shard_map/ppermute | solution.py:43
  228.7 2.3 copy-start.1
  228.7 25.1 %collective-permute-start.4 = (bf16[4096,128]{0,1:T(8,128)(2,1)S(1)}, bf16[4096,128]{0,1:T(8,128)(2,1)}, u32[]{:S(2)}, u32[]{:S(2)}) collective-permute-start(bf16[4096,128]{0,1:T(8,128)(2,1)S(1)} %maximum_select_fusion.2), channel_id=1, source_target_pairs={{0,16},{1,17},{2,18},{3,19},{4,20},{5,21},{6,22},{7,23},{8,24},{9,... | collective-permute-start | bytes 3145736 | tf_op jit(solution)/shard_map/ppermute | solution.py:43
  256.5 48.1 %collective-permute-start.5 = (bf16[8192,128]{0,1:T(8,128)(2,1)S(1)}, bf16[8192,128]{0,1:T(8,128)(2,1)}, u32[]{:S(2)}, u32[]{:S(2)}) collective-permute-start(bf16[8192,128]{0,1:T(8,128)(2,1)S(1)} %maximum_select_fusion.1), channel_id=1, source_target_pairs={{0,32},{1,33},{2,34},{3,35},{4,36},{5,37},{6,38},{7,39},{8,40},{9,... | collective-permute-start | bytes 6291464 | tf_op jit(solution)/shard_map/ppermute | solution.py:43
  315.5 6.7 %copy-start.4 = (s32[1,24]{1,0:T(1,128)S(1)}, s32[1,24]{1,0:T(1,128)}, u32[]{:S(2)}) copy-start(s32[1,24]{1,0:T(1,128)} %param.12) | copy-start | bytes 292
  318.4 4.5 copy-start.2
  318.5 4.5 copy-start.5
Sparse Core Ops, SparseCore 0:
  327.2 277.9 all-reduce.2
